TPU v7x, 128 devices: a whole 4x4x4 slice. The times are simulated.
128 devices in a mesh: ctx: 16 (over z, y_hi, core), exp: 8 (over x, y_lo).
Axes of the slice: x: 4, y: 4 (y_hi: 2, y_lo: 2; y = y_hi * 2 + y_lo), z: 4, core: 2. Of those that a mesh axis runs over, the one named last changes fastest.
Arguments:
- tokens: bfloat16 [16384, 2048], P(('ctx', 'exp')), may hold values from -12 to 12
- ln1_gain: float32 [2048], replicated, may hold values from 0.5 to 2
- w_query: bfloat16 [2048, 2048], P(None, 'exp')
- key_weight: bfloat16 [2048, 256], replicated
- value_weight: bfloat16 [2048, 256], replicated, may hold values from -0.125 to 0.125
- q_gain: float32 [128], replicated, may hold values from 0.5 to 5.5
- k_gain: float32 [128], replicated, may hold values from 0.5 to 5.5
- w_out: bfloat16 [2048, 2048], P('exp'), may hold values from -0.125 to 0.125
- ln2_gain: float32 [2048], replicated, may hold values from 0.5 to 2
- expert_ids: int32 [16384, 8], P(('ctx', 'exp')), may hold values from 0 to 127, all different within a row; in each aligned block of 128 rows (0 to 127, 128 to 255, ...) at most 12 rows name the same one
- route_weights: int32 [16384, 8], P(('ctx', 'exp')), may hold values from 1 to 255
- w_gate: bfloat16 [128, 2048, 768], P(('ctx', 'exp')), may hold values from -0.125 to 0.125
- w_up: bfloat16 [128, 2048, 768], P(('ctx', 'exp')), may hold values from -0.125 to 0.125
- w_down: bfloat16 [128, 768, 2048], P(('ctx', 'exp')), may hold values from -0.21875 to 0.21875
Outputs:
- layer_out: bfloat16 [16384, 2048], P(('ctx', 'exp'))
Inputs may be any that keep to these rules, and one draw needn't show every extreme that they name: `expert_ids`: each token names 8 different experts; among the 128 rows of one device no expert is named by more than 12 rows. `route_weights`: a choice weighs the value divided by 1024.
All inputs are finite; a program needn't handle non-finite values.
Results may differ from a plain program's by a relative error of at most 0.02.
The roundings to bfloat16 on the way count: a program that leaves them out, or rounds other values in their place, can miss the bound.
Values may be sent and summed in bfloat16 or wider, within the bound.
A program may use at most 128 MiB of HBM per device.

v0:
```python
import jax
import jax.numpy as jnp
from jax import lax
from jax.sharding import PartitionSpec as P

HEAD_SIZE = 128
QUERY_HEADS = 16
KEY_VALUE_HEADS = 2
TOP = 8
eps_value = 1e-06
theta_value = 1000000.0
floor_value = -1e30
block_span = 1024


def rms_scale(value_states, norm_gain):
    return (
        value_states
        * lax.rsqrt(jnp.mean(value_states * value_states, axis=-1, keepdims=True) + eps_value)
        * norm_gain
    )


def rotate(value_states, positions):
    half_size = value_states.shape[-1] // 2
    frequency = theta_value ** (
        -2.0 * jnp.arange(half_size, dtype=jnp.float32) / value_states.shape[-1]
    )
    angles = positions.astype(jnp.float32)[:, None] * frequency[None, :]
    cosine = jnp.cos(angles)
    sine_part = jnp.sin(angles)
    leading = value_states[..., :half_size]
    second = value_states[..., half_size:]
    return jnp.concatenate(
        [leading * cosine - second * sine_part, second * cosine + leading * sine_part], axis=-1
    )


def attend_block(carried, group_queries, group_first, key_rows, value_rows, key_first):
    running_max, running_sum, weighted = carried
    scores = jnp.einsum(
        "hqd,kd->hqk", group_queries, key_rows, preferred_element_type=jnp.float32
    ) * group_queries.shape[-1] ** (-0.5)
    query_pos = group_first + jnp.arange(group_queries.shape[1])
    key_pos = key_first + jnp.arange(key_rows.shape[0])
    visible = key_pos[None, :] <= query_pos[:, None]
    scores = jnp.where(visible[None], scores, -jnp.inf)
    new_max = jnp.maximum(running_max, jnp.max(scores, axis=-1))
    weights = jnp.exp(scores - new_max[..., None])
    rescale = jnp.exp(running_max - new_max)
    running_sum = running_sum * rescale + jnp.sum(weights, axis=-1)
    weighted = weighted * rescale[..., None] + jnp.einsum(
        "hqk,kd->hqd", weights.astype(jnp.bfloat16), value_rows, preferred_element_type=jnp.float32
    )
    return (new_max, running_sum, weighted)


def scan_keys(group_state, group_queries, group_first, key_rows, value_rows, step_rows):
    group_last = group_first + group_queries.shape[1] - 1

    def one_block(block_index, carried):
        key_first = block_index * step_rows
        key_part = lax.dynamic_slice_in_dim(key_rows, block_index * step_rows, step_rows, 0)
        value_part = lax.dynamic_slice_in_dim(value_rows, block_index * step_rows, step_rows, 0)
        return lax.cond(
            key_first > group_last,
            lambda current: current,
            lambda current: attend_block(
                current, group_queries, group_first, key_part, value_part, key_first
            ),
            carried,
        )

    return lax.fori_loop(0, key_rows.shape[0] // step_rows, one_block, group_state)


def shards(
    tokens,
    ln1_gain,
    w_query,
    key_weight,
    value_weight,
    q_gain,
    k_gain,
    w_out,
    ln2_gain,
    expert_ids,
    route_weights,
    w_gate,
    w_up,
    w_down,
):
    rows_dev = tokens.shape[0]
    ctx_count = lax.axis_size("ctx")
    exp_count = lax.axis_size("exp")
    ctx_rows = rows_dev * exp_count
    heads_dev = w_query.shape[1] // HEAD_SIZE
    group_width = QUERY_HEADS // KEY_VALUE_HEADS
    kv_head = lax.axis_index("exp") * heads_dev // group_width
    inputs32 = tokens.astype(jnp.float32)
    normed_input = rms_scale(inputs32, ln1_gain).astype(jnp.bfloat16)
    key_cols = lax.dynamic_slice_in_dim(key_weight, kv_head * HEAD_SIZE, HEAD_SIZE, 1)
    value_cols = lax.dynamic_slice_in_dim(value_weight, kv_head * HEAD_SIZE, HEAD_SIZE, 1)
    joined = jnp.concatenate([w_query, key_cols, value_cols], axis=1)
    projected = jnp.dot(
        lax.all_gather(normed_input, "exp", axis=0, tiled=True),
        joined,
        preferred_element_type=jnp.float32,
    )
    ctx_first = lax.axis_index("ctx") * ctx_rows
    positions = ctx_first + jnp.arange(ctx_rows)
    query_cols = heads_dev * HEAD_SIZE
    query_heads = (
        projected[:, :query_cols].reshape(ctx_rows, heads_dev, HEAD_SIZE).transpose(1, 0, 2)
    )
    queries = rotate(rms_scale(query_heads, q_gain), positions).astype(jnp.bfloat16)
    keys_all = rotate(
        rms_scale(projected[:, query_cols : query_cols + HEAD_SIZE], k_gain), positions
    ).astype(jnp.bfloat16)
    values_all = projected[:, query_cols + HEAD_SIZE :].astype(jnp.bfloat16)
    groups = ((queries, ctx_first),)
    initial = tuple(
        (
            (
                jnp.full((heads_dev, group_queries.shape[1]), floor_value, jnp.float32),
                jnp.zeros((heads_dev, group_queries.shape[1]), jnp.float32),
                jnp.zeros((heads_dev, group_queries.shape[1], HEAD_SIZE), jnp.float32),
            )
            for group_queries, group_first in groups
        )
    )
    key_rows = lax.all_gather(keys_all, "ctx", axis=0, tiled=True)
    value_rows = lax.all_gather(values_all, "ctx", axis=0, tiled=True)
    finals = tuple(
        (
            scan_keys(group_state, group_queries, group_first, key_rows, value_rows, block_span)
            for (group_queries, group_first), group_state in zip(groups, initial)
        )
    )
    outputs = [
        (weighted / running_sum[..., None]).astype(jnp.bfloat16)
        for running_max, running_sum, weighted in finals
    ]
    merged = outputs[0]
    attended = merged.transpose(1, 0, 2).reshape(ctx_rows, query_cols)
    attention = lax.psum_scatter(
        jnp.dot(attended, w_out, preferred_element_type=jnp.float32).astype(jnp.bfloat16),
        "exp",
        scatter_dimension=0,
        tiled=True,
    ).astype(jnp.float32)
    residual = (inputs32 + attention).astype(jnp.bfloat16)
    normed2 = rms_scale(residual.astype(jnp.float32), ln2_gain).astype(jnp.bfloat16)
    experts = ctx_count * exp_count
    capacity = max(2, 3 * rows_dev * TOP // (2 * experts))
    chosen = expert_ids[:, :, None] == jnp.arange(experts)[None, None, :]
    counts = jnp.sum(chosen, axis=1, dtype=jnp.int32)
    rank_table = jnp.cumsum(counts, axis=0, dtype=jnp.int32) - counts
    slot_index = jnp.sum(jnp.where(chosen, rank_table[:, None, :], 0), axis=2)
    slot_hot = slot_index[:, :, None] == jnp.arange(capacity)[None, None, :]
    dispatch = jnp.einsum(
        "tke,tkc->ect",
        chosen.astype(jnp.bfloat16),
        slot_hot.astype(jnp.bfloat16),
        preferred_element_type=jnp.float32,
    ).astype(jnp.bfloat16)
    outgoing = jnp.einsum(
        "ect,td->ecd", dispatch, normed2, preferred_element_type=jnp.float32
    ).astype(jnp.bfloat16)
    weight_frac = route_weights.astype(jnp.float32) / 1024.0
    combine = jnp.einsum(
        "tke,tkc->tec",
        chosen.astype(jnp.float32) * weight_frac[:, :, None],
        slot_hot.astype(jnp.float32),
    ).astype(jnp.bfloat16)
    width = outgoing.shape[2]
    arrived = lax.all_to_all(outgoing, ("ctx", "exp"), split_axis=0, concat_axis=0, tiled=True)
    flat_rows = arrived.reshape(-1, width)
    gate_act = jnp.dot(flat_rows, w_gate[0], preferred_element_type=jnp.float32)
    up_act = jnp.dot(flat_rows, w_up[0], preferred_element_type=jnp.float32)
    hidden = (jax.nn.silu(gate_act) * up_act).astype(jnp.bfloat16)
    produced = jnp.dot(hidden, w_down[0], preferred_element_type=jnp.float32).astype(jnp.bfloat16)
    returned = lax.all_to_all(
        produced.reshape(arrived.shape), ("ctx", "exp"), split_axis=0, concat_axis=0, tiled=True
    )
    mixture = jnp.einsum("tec,ecd->td", combine, returned, preferred_element_type=jnp.float32)
    return (residual.astype(jnp.float32) + mixture).astype(jnp.bfloat16)


def solution(mesh):
    in_specs = (
        P(("ctx", "exp"), None),
        P(),
        P(None, "exp"),
        P(),
        P(),
        P(),
        P(),
        P("exp", None),
        P(),
        P(("ctx", "exp"), None),
        P(("ctx", "exp"), None),
        P(("ctx", "exp"), None, None),
        P(("ctx", "exp"), None, None),
        P(("ctx", "exp"), None, None),
    )
    out_specs = P(("ctx", "exp"), None)
    return jax.shard_map(shards, mesh=mesh, in_specs=in_specs, out_specs=out_specs, check_vma=False)
```

profile of v0, /device:TPU:42, one launch (start us, length us, event | category | flops | bytes accessed | tf_op | source)
XLA Modules:
  0.0 804.0 jit_solution(13334901165268081912)
XLA Ops:
  7.9 2.0 fusion.42
  10.1 2.2 constant_dynamic-slice_fusion
  12.3 90.0 %all-gather.4.cloned.1.call-done = bf16[1024,2048]{1,0:T(8,128)(2,1)} async-done(((bf16[128,2048]{1,0:T(8,128)(2,1)}), bf16[1024,2048]{1,0:T(8,128)(2,1)}) %all-gather.4.cloned.1.call-update) | async-done | bytes 4194320 | tf_op jit(solution)/shard_map/all_gather | solution.py:106
  102.3 5.2 fusion.33
  113.4 2.3 slice.32
  115.8 2.5 copy.36
  127.2 39.6 %all-gather.6.cloned.1.call-done = bf16[16384,128]{0,1:T(8,128)(2,1)} async-done(((bf16[1024,128]{0,1:T(8,128)(2,1)}), bf16[16384,128]{0,1:T(8,128)(2,1)}) %all-gather.6.cloned.1.call-update) | async-done | bytes 4194320 | tf_op jit(solution)/shard_map/all_gather | solution.py:132
  166.8 6.6 copy.39
  173.5 49.0 %all-gather.8.cloned.1.call-done = bf16[16384,128]{0,1:T(8,128)(2,1)} async-done(((bf16[1024,128]{0,1:T(8,128)(2,1)}), bf16[16384,128]{0,1:T(8,128)(2,1)}) %all-gather.8.cloned.1.call-update) | async-done | bytes 4194320 | tf_op jit(solution)/shard_map/all_gather | solution.py:133
  222.5 6.4 copy.40
  230.0 58.9 %while.17 = (s32[]{:T(128)}, f32[2,1024]{1,0:T(2,128)S(1)}, f32[2,1024]{1,0:T(2,128)S(1)}, f32[2,1024,128]{2,1,0:T(8,128)}, s32[]{:T(128)}, /*index=5*/s32[]{:T(...) while((s32[]{:T(128)}, f32[2,1024]{1,0:T(2,128)S(1)}, ...), condition=%wide.region_8.9_spmd, body=%wide.region_3.8_spmd.sunk | while | flops 1098389504 | bytes 45236608 | solution.py:74
  230.0 11.6 %conditional.2 = (f32[2,1024]{1,0:T(2,128)S(1)}, f32[2,1024]{1,0:T(2,128)S(1)}, f32[2,1024,128]{2,1,0:T(8,128)}) conditional(s32[]{:T(128)} %convert_element_type.167, (s32[]{:T(128)}, s32[]{:T(128)}, bf16[16384,128]{1,0:T(8,128)(2,1)}, bf16[2,1024,128]{2,1,0:T(8,128)(2,1)}, f32[2,1024]{1,0:T(2,128)S(1)}, /*index=5*/f32[2,1024]{1,0:T(2,128)S(1)}, ...), branch_computations={%region_4.6_spmd, %region_7.7_spmd} | conditional | flops 1098389504 | bytes 45219996 | solution.py:65
  231.7 3.3 fusion.2
  235.0 2.0 fusion.1
  237.0 3.6 fusion.6
  241.7 11.6 %conditional.2 = (f32[2,1024]{1,0:T(2,128)S(1)}, f32[2,1024]{1,0:T(2,128)S(1)}, f32[2,1024,128]{2,1,0:T(8,128)}) conditional(s32[]{:T(128)} %convert_element_type.167, (s32[]{:T(128)}, s32[]{:T(128)}, bf16[16384,128]{1,0:T(8,128)(2,1)}, bf16[2,1024,128]{2,1,0:T(8,128)(2,1)}, f32[2,1024]{1,0:T(2,128)S(1)}, /*index=5*/f32[2,1024]{1,0:T(2,128)S(1)}, ...), branch_computations={%region_4.6_spmd, %region_7.7_spmd} | conditional | flops 1098389504 | bytes 45219996 | solution.py:65
  243.3 3.3 fusion.2
  246.6 2.0 fusion.1
  248.6 3.6 fusion.6
  253.3 11.6 %conditional.2 = (f32[2,1024]{1,0:T(2,128)S(1)}, f32[2,1024]{1,0:T(2,128)S(1)}, f32[2,1024,128]{2,1,0:T(8,128)}) conditional(s32[]{:T(128)} %convert_element_type.167, (s32[]{:T(128)}, s32[]{:T(128)}, bf16[16384,128]{1,0:T(8,128)(2,1)}, bf16[2,1024,128]{2,1,0:T(8,128)(2,1)}, f32[2,1024]{1,0:T(2,128)S(1)}, /*index=5*/f32[2,1024]{1,0:T(2,128)S(1)}, ...), branch_computations={%region_4.6_spmd, %region_7.7_spmd} | conditional | flops 1098389504 | bytes 45219996 | solution.py:65
  254.9 3.3 fusion.2
  258.3 2.0 fusion.1
  260.3 3.6 fusion.6
  264.9 11.6 %conditional.2 = (f32[2,1024]{1,0:T(2,128)S(1)}, f32[2,1024]{1,0:T(2,128)S(1)}, f32[2,1024,128]{2,1,0:T(8,128)}) conditional(s32[]{:T(128)} %convert_element_type.167, (s32[]{:T(128)}, s32[]{:T(128)}, bf16[16384,128]{1,0:T(8,128)(2,1)}, bf16[2,1024,128]{2,1,0:T(8,128)(2,1)}, f32[2,1024]{1,0:T(2,128)S(1)}, /*index=5*/f32[2,1024]{1,0:T(2,128)S(1)}, ...), branch_computations={%region_4.6_spmd, %region_7.7_spmd} | conditional | flops 1098389504 | bytes 45219996 | solution.py:65
  266.6 3.3 fusion.2
  269.9 2.0 fusion.1
  271.9 3.6 fusion.6
  276.6 11.6 %conditional.2 = (f32[2,1024]{1,0:T(2,128)S(1)}, f32[2,1024]{1,0:T(2,128)S(1)}, f32[2,1024,128]{2,1,0:T(8,128)}) conditional(s32[]{:T(128)} %convert_element_type.167, (s32[]{:T(128)}, s32[]{:T(128)}, bf16[16384,128]{1,0:T(8,128)(2,1)}, bf16[2,1024,128]{2,1,0:T(8,128)(2,1)}, f32[2,1024]{1,0:T(2,128)S(1)}, /*index=5*/f32[2,1024]{1,0:T(2,128)S(1)}, ...), branch_computations={%region_4.6_spmd, %region_7.7_spmd} | conditional | flops 1098389504 | bytes 45219996 | solution.py:65
  278.2 3.3 fusion.2
  281.6 2.0 fusion.1
  283.6 3.6 fusion.6
  288.9 2.5 copy.41
  292.8 4.5 convolution_convert_fusion.2
  297.8 2.4 select_reduce_fusion
  300.2 2.3 fusion.39
  302.5 211.1 %reduce-scatter.2.cloned.1.call-done = bf16[128,2048]{1,0:T(8,128)(2,1)} async-done(((bf16[1024,2048]{1,0:T(8,128)(2,1)}), bf16[128,2048]{1,0:T(8,128)(2,1)}) %reduce-scatter.2.cloned.1.call-update) | async-done | bytes 524304 | tf_op jit(solution)/shard_map/reduce_scatter | solution.py:146
  515.1 3.2 convolution_convert_fusion.1
  518.4 6.9 copy.45
  525.2 104.3 %all_to_all.10 = bf16[128,12,2048]{2,1,0:T(8,128)(2,1)} all-to-all(bf16[128,12,2048]{2,1,0:T(8,128)(2,1)} %copy.45), channel_id=1, replica_groups=mesh['ctx'=16,'exp'=8] {'ctx','exp'}, dimensions={0} | all-to-all | bytes 12582912 | tf_op jit(solution)/shard_map/all_to_all | solution.py:177
  629.5 10.7 %reshape.167 = bf16[1536,2048]{1,0:T(8,128)(2,1)} reshape(bf16[128,12,2048]{2,1,0:T(8,128)(2,1)} %all_to_all.10) | data formatting | bytes 12582912 | tf_op jit(solution)/shard_map/reshape | solution.py:178
  640.2 8.2 %fusion.22 = f32[1536,768]{1,0:T(8,128)S(1)} fusion(bf16[1536,2048]{1,0:T(8,128)(2,1)} %reshape.167, bf16[1,2048,768]{2,1,0:T(8,128)(2,1)} %param.29), kind=kOutput, calls=%fused_computation.30 | convolution fusion | flops 4831838208 | bytes 14155776 | tf_op jit(solution)/shard_map/dot_general | solution.py:179
  648.4 5.6 multiply_convert_fusion
  654.0 7.1 convolution_convert_fusion
  661.1 10.6 %reshape.168 = bf16[128,12,2048]{2,1,0:T(8,128)(2,1)} reshape(bf16[1536,2048]{1,0:T(8,128)(2,1)} %convolution_convert_fusion) | data formatting | bytes 12582912 | tf_op jit(solution)/shard_map/reshape | solution.py:184
  671.7 10.3 %all-to-all-start.1 = ((bf16[128,12,2048]{2,1,0:T(8,128)(2,1)}), bf16[128,12,2048]{2,1,0:T(8,128)(2,1)}, u32[]{:S(2)}, u32[]{:S(2)}) async-start(bf16[128,12,2048]{2,1,0:T(8,128)(2,1)} %reshape.168), calls=%async_computation.2 | async-start | bytes 16777216 | tf_op jit(solution)/shard_map/all_to_all | solution.py:183
  682.2 2.0 convolution_convert_fusion.3
  684.1 101.5 %all-to-all-done.1 = bf16[128,12,2048]{2,1,0:T(8,128)(2,1)} async-done(((bf16[128,12,2048]{2,1,0:T(8,128)(2,1)}), bf16[128,12,2048]{2,1,0:T(8,128)(2,1)}, u32[]{:S(2)}, u32[]{:S(2)}) %all-to-all-start.1) | async-done | bytes 6291488 | tf_op jit(solution)/shard_map/all_to_all | solution.py:183
  785.6 11.6 %fusion.30 = bf16[128,2048]{1,0:T(8,128)(2,1)} fusion(bf16[128,12,2048]{2,1,0:T(8,128)(2,1)} %all-to-all-done.1, bf16[128,128,12]{1,2,0:T(8,128)(2,1)} %convolution_convert_fusion.3, bf16[128,2048]{1,0:T(8,128)(2,1)} %reduce-scatter.2.cloned.1.call-done, bf16[128,2048]{1,0:T(8,128)(2,1)} %param.18), kind=kOutput, calls=%fused_computation.34 | convolution fusion | flops 807141376 | bytes 8257536 | tf_op jit(solution)/shard_map/tec,ecd->td/dot_general | solution.py:186
  (143 shorter events, 34.7 us)
Async XLA Ops:
  6.5 647.5 %copy-start = (bf16[1,768,2048]{2,1,0:T(8,128)(2,1)S(1)}, bf16[1,768,2048]{2,1,0:T(8,128)(2,1)}, u32[]{:S(2)}) copy-start(bf16[1,768,2048]{2,1,0:T(8,128)(2,1)} %param.31) | copy-start | bytes 9437188
  6.5 95.8 %all-gather.4.cloned.1.call-start = ((), (), s32[]{:S(2)}) async-start(), calls=%async_computation.3 | async-start | bytes 4718592 | tf_op jit(solution)/shard_map/all_gather | solution.py:106
  10.0 156.8 %all-gather.6.cloned.1.call-start = ((), (), s32[]{:S(2)}) async-start(), calls=%async_computation.4 | async-start | bytes 4456448 | tf_op jit(solution)/shard_map/all_gather | solution.py:132
  102.3 6.6 copy-start.9
  107.5 1.4 copy-start.5
  109.0 13.9 %copy-start.10 = (f32[128]{0:T(128)S(1)}, f32[128]{0:T(128)}, u32[]{:S(2)}) copy-start(f32[128]{0:T(128)} %param.23) | copy-start | bytes 1540
  111.5 111.0 %all-gather.8.cloned.1.call-start = ((), (), s32[]{:S(2)}) async-start(), calls=%async_computation.5 | async-start | bytes 4456448 | tf_op jit(solution)/shard_map/all_gather | solution.py:133
  113.4 400.2 %reduce-scatter.2.cloned.1.call-start = ((), (), s32[]{:S(2)}) async-start(), calls=%async_computation.6 | async-start | bytes 4718592 | tf_op jit(solution)/shard_map/reduce_scatter | solution.py:146
  231.7 3.3 copy-start.1
  235.0 2.0 copy-start.3
  240.6 1.1 copy-start.4
  243.3 3.3 copy-start.1
  246.6 2.0 copy-start.3
  252.2 1.1 copy-start.4
  254.9 3.3 copy-start.1
  258.3 2.0 copy-start.3
  263.9 1.1 copy-start.4
  266.6 3.3 copy-start.1
  269.9 2.0 copy-start.3
  275.5 1.1 copy-start.4
  278.2 3.3 copy-start.1
  281.5 2.0 copy-start.3
  287.2 1.1 copy-start.4
  292.8 4.5 copy-start.7
  297.3 217.8 %copy-start.6 = (f32[2048]{0:T(1024)S(1)}, f32[2048]{0:T(1024)}, u32[]{:S(2)}) copy-start(f32[2048]{0:T(1024)} %param.26) | copy-start | bytes 24580
  640.2 8.2 %copy-start.2 = (bf16[1536,2048]{1,0:T(8,128)(2,1)S(1)}, bf16[1536,2048]{1,0:T(8,128)(2,1)}, u32[]{:S(2)}) copy-start(bf16[1536,2048]{1,0:T(8,128)(2,1)} %reshape.167) | copy-start | bytes 18874372
  640.2 8.2 %copy-start.11 = (bf16[1,2048,768]{2,1,0:T(8,128)(2,1)S(1)}, bf16[1,2048,768]{2,1,0:T(8,128)(2,1)}, u32[]{:S(2)}) copy-start(bf16[1,2048,768]{2,1,0:T(8,128)(2,1)} %param.30) | copy-start | bytes 9437188
  671.7 10.3 %copy-start.8 = (s32[128,8]{0,1:T(8,128)S(1)}, s32[128,8]{0,1:T(8,128)}, u32[]{:S(2)}) copy-start(s32[128,8]{0,1:T(8,128)} %param.28) | copy-start | bytes 12292
  671.7 113.9 %all-to-all-start.1 = ((bf16[128,12,2048]{2,1,0:T(8,128)(2,1)}), bf16[128,12,2048]{2,1,0:T(8,128)(2,1)}, u32[]{:S(2)}, u32[]{:S(2)}) async-start(bf16[128,12,2048]{2,1,0:T(8,128)(2,1)} %reshape.168), calls=%async_computation.2 | async-start | bytes 16777216 | tf_op jit(solution)/shard_map/all_to_all | solution.py:183
Sparse Core Ops, SparseCore 0:
  10.1 92.1 all-gather.3
  111.7 55.1 all-gather.5
  169.3 53.1 all-gather.7
  297.4 216.1 reduce-scatter.1
where the time goes:
time: 811 us; the launch traced here: 804 us
  waiting for transfers between devices  491 us (61%)
  blocking collectives  104 us (13%)
  matrix products  84.1 us (10%)
  local copies, waits for them, and re-layouts  63.6 us (8%)
  other arithmetic  35.8 us (4%)
  between operations  13.6 us (2%)
  starting transfers between devices  10.4 us (1%)
    reduce_scatter x1, waiting for transfers between devices, shards(): lax.psum_scatter(jnp.dot(attended, w_out, preferred_element_type=jnp.floa...  211 us
    all_to_all x1, blocking collectives, shards(): lax.all_to_all(outgoing, ('ctx', 'exp'), split_axis=0, concat_axis=0, til...  104 us
    all_to_all x1, waiting for transfers between devices, shards(): lax.all_to_all(produced.reshape(arrived.shape), ('ctx', 'exp'), split_axi...  101 us
    all_gather x1, waiting for transfers between devices, shards(): lax.all_gather(normed_input, 'exp', axis=0, tiled=True)  90 us
    all_gather x1, waiting for transfers between devices, shards(): value_rows = lax.all_gather(values_all, 'ctx', axis=0, tiled=True)  49 us
    all_gather x1, waiting for transfers between devices, shards(): key_rows = lax.all_gather(keys_all, 'ctx', axis=0, tiled=True)  39.6 us
    dot_general x5, matrix products, attend_block(): jnp.einsum('hqk,kd->hqd', weights.astype(jnp.bfloat16), value_rows, prefe...  17.9 us
    dot_general x5, matrix products, attend_block(): jnp.einsum('hqd,kd->hqk', group_queries, key_rows, preferred_element_type...  16.5 us
  transfers between devices with their start and end apart: 5, of which 5 were waited for; matrix products, arithmetic and copies ran while one was open for 4% of the time, Pallas kernels for 0%

commit v1 on v0

--- a/solution.py
+++ b/solution.py
@@ -129,8 +129,11 @@
             for group_queries, group_first in groups
         )
     )
-    key_rows = lax.all_gather(keys_all, "ctx", axis=0, tiled=True)
-    value_rows = lax.all_gather(values_all, "ctx", axis=0, tiled=True)
+    key_rows, value_rows = jnp.split(
+        lax.all_gather(jnp.concatenate([keys_all, values_all], axis=1), "ctx", axis=0, tiled=True),
+        [keys_all.shape[1]],
+        axis=1,
+    )
     finals = tuple(
         (
             scan_keys(group_state, group_queries, group_first, key_rows, value_rows, block_span)

time: 811 us -> 784 us (0.967)
  waiting for transfers between devices: 491 us -> 461 us
    all_gather x2 -> x1, waiting for transfers between devices: 88.6 us -> 59 us  [shards(): lax.all_gather(jnp.concatenate([keys_all, values_all], axis=1), 'ctx', ax...]
  transfers between devices with their start and end apart: 5 -> 4, of which waited for: 5 -> 4; matrix products, arithmetic and copies ran while one was open for 4% -> 3% of each run, Pallas kernels for 0% -> 0%
where the time goes in v1:
time: 784 us; the launch traced here: 778 us
  waiting for transfers between devices  461 us (59%)
  blocking collectives  104 us (13%)
  matrix products  84.1 us (11%)
  local copies, waits for them, and re-layouts  67.5 us (9%)
  other arithmetic  35.8 us (5%)
  between operations  13.6 us (2%)
  starting transfers between devices  10.4 us (1%)
    reduce_scatter x1, waiting for transfers between devices, shards(): lax.psum_scatter(jnp.dot(attended, w_out, preferred_element_type=jnp.floa...  210 us
    all_to_all x1, blocking collectives, shards(): lax.all_to_all(outgoing, ('ctx', 'exp'), split_axis=0, concat_axis=0, til...  104 us
    all_to_all x1, waiting for transfers between devices, shards(): lax.all_to_all(produced.reshape(arrived.shape), ('ctx', 'exp'), split_axi...  101 us
    all_gather x1, waiting for transfers between devices, shards(): lax.all_gather(normed_input, 'exp', axis=0, tiled=True)  90 us
    all_gather x1, waiting for transfers between devices, shards(): lax.all_gather(jnp.concatenate([keys_all, values_all], axis=1), 'ctx', ax...  59 us
    dot_general x5, matrix products, attend_block(): jnp.einsum('hqk,kd->hqd', weights.astype(jnp.bfloat16), value_rows, prefe...  18 us
    dot_general x5, matrix products, attend_block(): jnp.einsum('hqd,kd->hqk', group_queries, key_rows, preferred_element_type...  16.5 us
  transfers between devices with their start and end apart: 4, of which 4 were waited for; matrix products, arithmetic and copies ran while one was open for 3% of the time, Pallas kernels for 0%

profile of v1, /device:TPU:42, one launch (start us, length us, event | category | flops | bytes accessed | tf_op | source)
XLA Modules:
  0.0 777.7 jit_solution(4211398964917344859)
XLA Ops:
  7.9 2.0 fusion.42
  10.1 2.3 constant_dynamic-slice_fusion
  12.3 90.0 %all-gather.3.cloned.1.call-done = bf16[1024,2048]{1,0:T(8,128)(2,1)} async-done(((bf16[128,2048]{1,0:T(8,128)(2,1)}), bf16[1024,2048]{1,0:T(8,128)(2,1)}) %all-gather.3.cloned.1.call-update) | async-done | bytes 4194320 | tf_op jit(solution)/shard_map/all_gather | solution.py:106
  102.3 5.2 fusion.33
  111.7 2.3 slice.33
  114.0 2.6 copy.36
  125.5 59.0 %all-gather.5.cloned.1.call-done = bf16[16384,256]{0,1:T(8,128)(2,1)} async-done(((bf16[1024,256]{0,1:T(8,128)(2,1)}), bf16[16384,256]{0,1:T(8,128)(2,1)}) %all-gather.5.cloned.1.call-update) | async-done | bytes 8388624 | tf_op jit(solution)/shard_map/all_gather | solution.py:133
  184.6 6.1 fusion.65
  190.6 6.4 copy.39
  197.0 6.4 copy.40
  204.5 58.8 %while.17 = (s32[]{:T(128)}, f32[2,1024]{1,0:T(2,128)S(1)}, f32[2,1024]{1,0:T(2,128)S(1)}, f32[2,1024,128]{2,1,0:T(8,128)}, s32[]{:T(128)}, /*index=5*/s32[]{:T(...) while((s32[]{:T(128)}, f32[2,1024]{1,0:T(2,128)S(1)}, ...), condition=%wide.region_8.9_spmd, body=%wide.region_3.8_spmd.sunk | while | flops 1098389504 | bytes 45236608 | solution.py:74
  204.5 11.6 %conditional.2 = (f32[2,1024]{1,0:T(2,128)S(1)}, f32[2,1024]{1,0:T(2,128)S(1)}, f32[2,1024,128]{2,1,0:T(8,128)}) conditional(s32[]{:T(128)} %convert_element_type.167, (s32[]{:T(128)}, s32[]{:T(128)}, bf16[16384,128]{1,0:T(8,128)(2,1)}, bf16[2,1024,128]{2,1,0:T(8,128)(2,1)}, f32[2,1024]{1,0:T(2,128)S(1)}, /*index=5*/f32[2,1024]{1,0:T(2,128)S(1)}, ...), branch_computations={%region_4.6_spmd, %region_7.7_spmd} | conditional | flops 1098389504 | bytes 45219996 | solution.py:65
  206.1 3.3 fusion.2
  209.5 2.0 fusion.1
  211.5 3.6 fusion.6
  216.1 11.6 %conditional.2 = (f32[2,1024]{1,0:T(2,128)S(1)}, f32[2,1024]{1,0:T(2,128)S(1)}, f32[2,1024,128]{2,1,0:T(8,128)}) conditional(s32[]{:T(128)} %convert_element_type.167, (s32[]{:T(128)}, s32[]{:T(128)}, bf16[16384,128]{1,0:T(8,128)(2,1)}, bf16[2,1024,128]{2,1,0:T(8,128)(2,1)}, f32[2,1024]{1,0:T(2,128)S(1)}, /*index=5*/f32[2,1024]{1,0:T(2,128)S(1)}, ...), branch_computations={%region_4.6_spmd, %region_7.7_spmd} | conditional | flops 1098389504 | bytes 45219996 | solution.py:65
  217.7 3.3 fusion.2
  221.1 2.0 fusion.1
  223.1 3.6 fusion.6
  227.7 11.6 %conditional.2 = (f32[2,1024]{1,0:T(2,128)S(1)}, f32[2,1024]{1,0:T(2,128)S(1)}, f32[2,1024,128]{2,1,0:T(8,128)}) conditional(s32[]{:T(128)} %convert_element_type.167, (s32[]{:T(128)}, s32[]{:T(128)}, bf16[16384,128]{1,0:T(8,128)(2,1)}, bf16[2,1024,128]{2,1,0:T(8,128)(2,1)}, f32[2,1024]{1,0:T(2,128)S(1)}, /*index=5*/f32[2,1024]{1,0:T(2,128)S(1)}, ...), branch_computations={%region_4.6_spmd, %region_7.7_spmd} | conditional | flops 1098389504 | bytes 45219996 | solution.py:65
  229.4 3.3 fusion.2
  232.7 2.0 fusion.1
  234.7 3.6 fusion.6
  239.4 11.6 %conditional.2 = (f32[2,1024]{1,0:T(2,128)S(1)}, f32[2,1024]{1,0:T(2,128)S(1)}, f32[2,1024,128]{2,1,0:T(8,128)}) conditional(s32[]{:T(128)} %convert_element_type.167, (s32[]{:T(128)}, s32[]{:T(128)}, bf16[16384,128]{1,0:T(8,128)(2,1)}, bf16[2,1024,128]{2,1,0:T(8,128)(2,1)}, f32[2,1024]{1,0:T(2,128)S(1)}, /*index=5*/f32[2,1024]{1,0:T(2,128)S(1)}, ...), branch_computations={%region_4.6_spmd, %region_7.7_spmd} | conditional | flops 1098389504 | bytes 45219996 | solution.py:65
  241.0 3.3 fusion.2
  244.3 2.0 fusion.1
  246.3 3.6 fusion.6
  251.0 11.6 %conditional.2 = (f32[2,1024]{1,0:T(2,128)S(1)}, f32[2,1024]{1,0:T(2,128)S(1)}, f32[2,1024,128]{2,1,0:T(8,128)}) conditional(s32[]{:T(128)} %convert_element_type.167, (s32[]{:T(128)}, s32[]{:T(128)}, bf16[16384,128]{1,0:T(8,128)(2,1)}, bf16[2,1024,128]{2,1,0:T(8,128)(2,1)}, f32[2,1024]{1,0:T(2,128)S(1)}, /*index=5*/f32[2,1024]{1,0:T(2,128)S(1)}, ...), branch_computations={%region_4.6_spmd, %region_7.7_spmd} | conditional | flops 1098389504 | bytes 45219996 | solution.py:65
  252.6 3.3 fusion.2
  255.9 2.0 fusion.1
  257.9 3.6 fusion.6
  263.3 2.5 copy.41
  267.1 4.5 convolution_convert_fusion.2
  272.2 2.4 select_reduce_fusion
  274.6 2.3 fusion.39
  276.9 210.5 %reduce-scatter.2.cloned.1.call-done = bf16[128,2048]{1,0:T(8,128)(2,1)} async-done(((bf16[1024,2048]{1,0:T(8,128)(2,1)}), bf16[128,2048]{1,0:T(8,128)(2,1)}) %reduce-scatter.2.cloned.1.call-update) | async-done | bytes 524304 | tf_op jit(solution)/shard_map/reduce_scatter | solution.py:149
  488.9 3.2 convolution_convert_fusion.1
  492.1 6.8 copy.45
  499.0 104.3 %all_to_all.10 = bf16[128,12,2048]{2,1,0:T(8,128)(2,1)} all-to-all(bf16[128,12,2048]{2,1,0:T(8,128)(2,1)} %copy.45), channel_id=1, replica_groups=mesh['ctx'=16,'exp'=8] {'ctx','exp'}, dimensions={0} | all-to-all | bytes 12582912 | tf_op jit(solution)/shard_map/all_to_all | solution.py:180
  603.3 10.7 %reshape.167 = bf16[1536,2048]{1,0:T(8,128)(2,1)} reshape(bf16[128,12,2048]{2,1,0:T(8,128)(2,1)} %all_to_all.10) | data formatting | bytes 12582912 | tf_op jit(solution)/shard_map/reshape | solution.py:181
  614.0 8.2 %fusion.22 = f32[1536,768]{1,0:T(8,128)S(1)} fusion(bf16[1536,2048]{1,0:T(8,128)(2,1)} %reshape.167, bf16[1,2048,768]{2,1,0:T(8,128)(2,1)} %param.29), kind=kOutput, calls=%fused_computation.30 | convolution fusion | flops 4831838208 | bytes 14155776 | tf_op jit(solution)/shard_map/dot_general | solution.py:182
  622.2 5.6 multiply_convert_fusion
  627.8 7.1 convolution_convert_fusion
  634.9 10.6 %reshape.168 = bf16[128,12,2048]{2,1,0:T(8,128)(2,1)} reshape(bf16[1536,2048]{1,0:T(8,128)(2,1)} %convolution_convert_fusion) | data formatting | bytes 12582912 | tf_op jit(solution)/shard_map/reshape | solution.py:187
  645.5 10.3 %all-to-all-start.1 = ((bf16[128,12,2048]{2,1,0:T(8,128)(2,1)}), bf16[128,12,2048]{2,1,0:T(8,128)(2,1)}, u32[]{:S(2)}, u32[]{:S(2)}) async-start(bf16[128,12,2048]{2,1,0:T(8,128)(2,1)} %reshape.168), calls=%async_computation.2 | async-start | bytes 16777216 | tf_op jit(solution)/shard_map/all_to_all | solution.py:186
  655.9 2.0 convolution_convert_fusion.3
  657.9 101.5 %all-to-all-done.1 = bf16[128,12,2048]{2,1,0:T(8,128)(2,1)} async-done(((bf16[128,12,2048]{2,1,0:T(8,128)(2,1)}), bf16[128,12,2048]{2,1,0:T(8,128)(2,1)}, u32[]{:S(2)}, u32[]{:S(2)}) %all-to-all-start.1) | async-done | bytes 6291488 | tf_op jit(solution)/shard_map/all_to_all | solution.py:186
  759.4 11.6 %fusion.30 = bf16[128,2048]{1,0:T(8,128)(2,1)} fusion(bf16[128,12,2048]{2,1,0:T(8,128)(2,1)} %all-to-all-done.1, bf16[128,128,12]{1,2,0:T(8,128)(2,1)} %convolution_convert_fusion.3, bf16[128,2048]{1,0:T(8,128)(2,1)} %reduce-scatter.2.cloned.1.call-done, bf16[128,2048]{1,0:T(8,128)(2,1)} %param.18), kind=kOutput, calls=%fused_computation.34 | convolution fusion | flops 807141376 | bytes 8257536 | tf_op jit(solution)/shard_map/tec,ecd->td/dot_general | solution.py:189
  (141 shorter events, 32.8 us)
Async XLA Ops:
  6.5 621.3 %copy-start = (bf16[1,768,2048]{2,1,0:T(8,128)(2,1)S(1)}, bf16[1,768,2048]{2,1,0:T(8,128)(2,1)}, u32[]{:S(2)}) copy-start(bf16[1,768,2048]{2,1,0:T(8,128)(2,1)} %param.31) | copy-start | bytes 9437188
  6.5 95.8 %all-gather.3.cloned.1.call-start = ((), (), s32[]{:S(2)}) async-start(), calls=%async_computation.3 | async-start | bytes 4718592 | tf_op jit(solution)/shard_map/all_gather | solution.py:106
  10.0 174.6 %all-gather.5.cloned.1.call-start = ((), (), s32[]{:S(2)}) async-start(), calls=%async_computation.4 | async-start | bytes 8912896 | tf_op jit(solution)/shard_map/all_gather | solution.py:133
  102.3 6.5 copy-start.9
  107.5 1.4 copy-start.5
  109.0 12.2 %copy-start.10 = (f32[128]{0:T(128)S(1)}, f32[128]{0:T(128)}, u32[]{:S(2)}) copy-start(f32[128]{0:T(128)} %param.23) | copy-start | bytes 1540
  111.6 375.8 %reduce-scatter.2.cloned.1.call-start = ((), (), s32[]{:S(2)}) async-start(), calls=%async_computation.5 | async-start | bytes 4718592 | tf_op jit(solution)/shard_map/reduce_scatter | solution.py:149
  206.1 3.3 copy-start.1
  209.5 2.0 copy-start.3
  215.1 1.0 copy-start.4
  217.7 3.3 copy-start.1
  221.1 2.0 copy-start.3
  226.7 1.0 copy-start.4
  229.4 3.3 copy-start.1
  232.7 2.0 copy-start.3
  238.3 1.0 copy-start.4
  241.0 3.3 copy-start.1
  244.3 2.0 copy-start.3
  249.9 1.0 copy-start.4
  252.6 3.3 copy-start.1
  255.9 2.0 copy-start.3
  261.5 1.0 copy-start.4
  267.1 4.5 copy-start.7
  271.6 217.2 %copy-start.6 = (f32[2048]{0:T(1024)S(1)}, f32[2048]{0:T(1024)}, u32[]{:S(2)}) copy-start(f32[2048]{0:T(1024)} %param.26) | copy-start | bytes 24580
  614.0 8.2 %copy-start.2 = (bf16[1536,2048]{1,0:T(8,128)(2,1)S(1)}, bf16[1536,2048]{1,0:T(8,128)(2,1)}, u32[]{:S(2)}) copy-start(bf16[1536,2048]{1,0:T(8,128)(2,1)} %reshape.167) | copy-start | bytes 18874372
  614.0 8.2 %copy-start.11 = (bf16[1,2048,768]{2,1,0:T(8,128)(2,1)S(1)}, bf16[1,2048,768]{2,1,0:T(8,128)(2,1)}, u32[]{:S(2)}) copy-start(bf16[1,2048,768]{2,1,0:T(8,128)(2,1)} %param.30) | copy-start | bytes 9437188
  645.5 10.3 %copy-start.8 = (s32[128,8]{0,1:T(8,128)S(1)}, s32[128,8]{0,1:T(8,128)}, u32[]{:S(2)}) copy-start(s32[128,8]{0,1:T(8,128)} %param.28) | copy-start | bytes 12292
  645.5 113.9 %all-to-all-start.1 = ((bf16[128,12,2048]{2,1,0:T(8,128)(2,1)}), bf16[128,12,2048]{2,1,0:T(8,128)(2,1)}, u32[]{:S(2)}, u32[]{:S(2)}) async-start(bf16[128,12,2048]{2,1,0:T(8,128)(2,1)} %reshape.168), calls=%async_computation.2 | async-start | bytes 16777216 | tf_op jit(solution)/shard_map/all_to_all | solution.py:186
Sparse Core Ops, SparseCore 0:
  10.1 92.1 all-gather.2
  111.8 72.7 all-gather.4
  271.8 215.5 reduce-scatter.1
